TPU v7x, 32 devices: a whole 2x2x4 slice. The times are simulated.
32 devices in a mesh: groups: 2 (over y), scan: 4 (over z), depth: 4 (over x, core).
Axes of the slice: x: 2, y: 2, z: 4, core: 2. Of those that a mesh axis runs over, the one named last changes fastest.
Arguments:
- probe: float32 [2, 256, 256], replicated, may hold values from -6 to 6
- slices: float32 [8, 2, 2048, 1024], P('depth', None, ('groups', 'scan')), parts along dimension 2, may hold values from -3 to 3, as said below
- positions: int32 [16, 2], P(('groups', 'scan')), parts along dimension 0, may hold values from 0 to 768, as said below
- counts: int32 [8], P(('groups', 'scan')), parts along dimension 0, may hold values from 1 to 2, as said below
- amplitude: float32 [16, 256, 256], P(('groups', 'scan')), parts along dimension 0, may hold values from 0.2 to 3
Outputs:
- gradient: float32 [8, 2, 2048, 1024], P('depth', None, ('groups', 'scan')), parts along dimension 2
There are 2 independent parts, one for each index of `groups`. A program takes and returns all parts, laid end to end along the dimension named above; an argument that names none is the same for every part. Nothing has to cross between parts.
Inputs may be any that keep to these rules, and one draw needn't show every extreme that they name: `positions`: row offsets lie in 0 to 255 and column offsets in 0 to 768; both ends of both ranges are taken. `counts`: each tile has 1 to 2 live patches, in its first slots; some tile has 2 and some has 1. `slices`: transmission of magnitude between exp(-1) and exp(1).
All inputs are finite; a program needn't handle non-finite values.
Results may differ from a plain program's by a relative error of at most 0.0003.
Values sent between devices are 32-bit elements; how exact they have to be, the bound alone decides.
A program may use at most 128 MiB of HBM per device.

v0:
```python
import math

import jax
import jax.numpy as jnp
from jax import lax
from jax.sharding import PartitionSpec as P

chirp_rate = 0.25


def shifted(block, axis, distance):
    devices = range(lax.axis_size(axis))
    route = [((i - distance) % len(devices), i) for i in devices]
    return lax.ppermute(block, axis, route)


def passed_along(block, axis, distance):
    devices = range(lax.axis_size(axis))
    route = [(i - distance, i) for i in devices if i - distance in devices]
    return lax.ppermute(block, axis, route)


def make_tables(length):
    index = jnp.arange(length, dtype=jnp.int32)
    product = index[:, None] * index[None, :] % length
    angle = 2.0 * math.pi / length * product.astype(jnp.float32)
    factor = 1.0 / math.sqrt(length)
    table_real = jnp.cos(angle) * factor
    table_imag = -jnp.sin(angle) * factor
    freq = jnp.where(index < length // 2, index, index - length).astype(jnp.float32)
    theta = -math.pi * chirp_rate / length * (freq[:, None] ** 2 + freq[None, :] ** 2)
    return (table_real, table_imag, jnp.cos(theta), jnp.sin(theta))


def left_product(matrix, field):
    return jnp.einsum(
        "jk,...kl->...jl",
        matrix,
        field,
        preferred_element_type=jnp.float32,
        precision=lax.Precision.HIGHEST,
    )


def right_product(field, matrix):
    return jnp.einsum(
        "...jk,kl->...jl",
        field,
        matrix,
        preferred_element_type=jnp.float32,
        precision=lax.Precision.HIGHEST,
    )


def transform(field, tables, forward):
    table_real = tables[0]
    table_imag = tables[1] if forward else -tables[1]
    real_part = field[..., 0, :, :]
    imag_part = field[..., 1, :, :]
    first_real = left_product(table_real, real_part) - left_product(table_imag, imag_part)
    first_imag = left_product(table_real, imag_part) + left_product(table_imag, real_part)
    out_real = right_product(first_real, table_real) - right_product(first_imag, table_imag)
    out_imag = right_product(first_real, table_imag) + right_product(first_imag, table_real)
    return jnp.stack([out_real, out_imag], axis=-3)


def complex_product(first, second, conjugate):
    first_real = first[..., 0, :, :]
    first_imag = first[..., 1, :, :]
    if conjugate:
        first_imag = -first_imag
    second_real = second[..., 0, :, :]
    second_imag = second[..., 1, :, :]
    return jnp.stack(
        [
            first_real * second_real - first_imag * second_imag,
            first_real * second_imag + first_imag * second_real,
        ],
        axis=-3,
    )


def propagate(field, tables, forward):
    spectrum = transform(field, tables, True)
    sine = tables[3] if forward else -tables[3]
    chirp = jnp.stack([tables[2], sine], axis=0)
    return transform(complex_product(spectrum, chirp, False), tables, False)


def far_field(exit_wave, measured, live, tables):
    spectrum = transform(exit_wave, tables, True)
    power = spectrum[..., 0, :, :] ** 2 + spectrum[..., 1, :, :] ** 2
    keep = live[:, None, None] * (1.0 - measured / jnp.sqrt(power + 1.0))
    residual = spectrum * keep[..., None, :, :]
    return transform(residual, tables, False)


def forward_local(wave_in, windows, tables):
    saved = []
    for layer in range(windows.shape[1]):
        psi = propagate(wave_in, tables, True)
        saved.append(psi)
        wave_in = complex_product(psi, windows[:, layer], False)
    return (wave_in, jnp.stack(saved, axis=1))


def adjoint_local(chi_wave, windows, saved, tables):
    terms = [None] * windows.shape[1]
    for layer in range(windows.shape[1] - 1, -1, -1):
        terms[layer] = complex_product(saved[:, layer], chi_wave, True)
        back = complex_product(windows[:, layer], chi_wave, True)
        chi_wave = propagate(back, tables, False)
    return (chi_wave, jnp.stack(terms, axis=1))


def body(probe, slices, positions, counts, amplitude):
    patch = probe.shape[-1]
    slots = positions.shape[0]
    layers = slices.shape[0]
    tables = make_tables(patch)
    depth_index = lax.axis_index("depth")
    depth_count = lax.axis_size("depth")
    last_group = depth_count - 1
    neighbour = shifted(slices, "scan", -1)
    extended = jnp.concatenate([slices, neighbour], axis=2)

    def cut_window(offset):
        zero = jnp.zeros((), jnp.int32)
        return lax.dynamic_slice(
            extended, (zero, zero, offset[0], offset[1]), (layers, 2, patch, patch)
        )

    windows = jax.vmap(cut_window)(positions)
    live = (jnp.arange(slots, dtype=jnp.int32) < counts[0]).astype(jnp.float32)
    wave_shape = (slots, 2, patch, patch)
    wave_now = jnp.broadcast_to(probe, wave_shape)
    saved = jnp.zeros((slots, layers, 2, patch, patch), jnp.float32)
    for step_number in range(depth_count):

        def advance(state):
            return forward_local(state[0], windows, tables)

        def passing(state):
            return state

        wave_now, saved = lax.cond(depth_index == step_number, advance, passing, (wave_now, saved))
        if step_number < depth_count - 1:
            wave_now = passed_along(wave_now, "depth", 1)
    chi_wave = lax.cond(
        depth_index == last_group,
        lambda waves: far_field(waves, amplitude, live, tables),
        lambda waves: jnp.zeros(wave_shape, jnp.float32),
        wave_now,
    )
    terms = jnp.zeros((slots, layers, 2, patch, patch), jnp.float32)
    for step_number in range(depth_count - 1, -1, -1):

        def retreat(state):
            return adjoint_local(state[0], windows, saved, tables)

        def keeping(state):
            return state

        chi_wave, terms = lax.cond(depth_index == step_number, retreat, keeping, (chi_wave, terms))
        if step_number > 0:
            chi_wave = passed_along(chi_wave, "depth", -1)
    grad_ext = jnp.zeros((layers, 2, 2 * patch, slices.shape[3]), jnp.float32)

    def add_slot(slot_index, grad_now):
        zero = jnp.zeros((), jnp.int32)
        start = (zero, zero, positions[slot_index, 0], positions[slot_index, 1])
        current = lax.dynamic_slice(grad_now, start, (layers, 2, patch, patch))
        return lax.dynamic_update_slice(grad_now, current + terms[slot_index], start)

    grad_ext = lax.fori_loop(0, slots, add_slot, grad_ext)
    margin = shifted(grad_ext[:, :, patch:], "scan", 1)
    return grad_ext[:, :, :patch] + margin


def solution(mesh):
    return jax.shard_map(
        body,
        mesh=mesh,
        in_specs=(
            P(),
            P("depth", None, ("groups", "scan"), None),
            P(("groups", "scan"), None),
            P(("groups", "scan")),
            P(("groups", "scan"), None, None),
        ),
        out_specs=P("depth", None, ("groups", "scan"), None),
        check_vma=False,
    )
```

profile of v0, /device:TPU:0, one launch (start us, length us, event | category | flops | bytes accessed | tf_op | source)
XLA Modules:
  0.0 634.2 jit_solution(11234639726278630442)
XLA Ops:
  0.0 5.0 collective-permute-start
  5.1 1.2 copy.243
  9.6 85.6 %collective-permute-done = f32[2,2,256,1024]{3,2,1,0:T(8,128)} collective-permute-done((f32[2,2,256,1024]{3,2,1,0:T(8,128)}, f32[2,2,256,1024]{3,2,1,0:T(8,128)}, u32[]{:S(2)}, u32[]{:S(2)}) %collective-permute-start) | collective-permute-done | bytes 4194336 | tf_op jit(solution)/shard_map/ppermute | solution.py:14
  95.2 8.5 %pad_maximum_fusion.16 = f32[2,2,512,1024]{3,2,1,0:T(8,128)} fusion(f32[2,2,256,1024]{3,2,1,0:T(8,128)} %collective-permute-done, f32[2,2,256,1024]{3,2,1,0:T(8,128)} %param.26), kind=kLoop, calls=%fused_computation.883 | loop fusion | flops 2097152 | bytes 16777216 | tf_op jit(solution)/shard_map/concatenate | solution.py:125
  103.7 7.2 %while.15 = (s32[]{:T(128)}, f32[2,2,512,1024]{3,2,1,0:T(8,128)}, s32[2,4]{1,0:T(2,128)S(1)}, f32[2,2,2,256,256]{4,3,2,1,0:T(8,128)S(1)}, s32[]{:T(128)}) while((s32[]{:T(128)}, f32[2,2,512,1024]{3,2,1,0:T(8,128)}, s32[2,4]{1,0:T(2,128)S(1)}, f32[2,2,2,256,256]{4,3,2,1,0:T(8,128)S(1)}, s32[]{:T(128)}) %tuple.214), condition=%wide.while_cond, body=%wide.while_body.sunk | while | flops 2 | bytes 2097285 | solution.py:129
  104.3 3.0 bitcast_dynamic-update-slice_fusion.2
  107.9 3.0 bitcast_dynamic-update-slice_fusion.2
  110.9 37.3 %conditional.9 = (f32[2,2,256,256]{3,2,0,1:T(8,128)}, f32[2,2,2,256,256]{4,3,0,2,1:T(8,128)}) conditional(s32[]{:T(128)} %convert_element_type.662, (f32[2,2,256,256]{2,3,0,1:T(8,128)}) %tuple.118, (f32[2,2,256,256]{2,3,0,1:T(8,128)}, f32[256,256]{1,0:T(8,128)S(1)}, f32[256,256]{1,0:T(8,128)S(1)}, f32[256,256]{1,0:T(8,128)S(1)}, ...), branch_computations={%region_0.1_spmd, %region_1.2_spmd} | conditional | flops 12893552640 | bytes 83361840 | solution.py:146
  111.2 1.7 fusion.8
  112.9 1.7 fusion.6
  125.0 1.2 fusion.49
  138.7 1.5 fusion.28
  146.6 1.5 pad_maximum_fusion
  148.2 2.5 copy.246
  150.7 2.3 collective-permute-start.1
  153.0 1.6 collective-permute-done.1
  154.6 10.7 %conditional.10 = (f32[2,2,2,256,256]{4,3,0,2,1:T(8,128)}, f32[2,2,256,256]{2,3,0,1:T(8,128)}) conditional(s32[]{:T(128)} %convert_element_type.663, (f32[2,2,256,256]{2,3,0,1:T(8,128)}, f32[2,2,2,256,256]{4,3,0,2,1:T(8,128)}) %tuple.88, (f32[2,2,256,256]{2,3,0,1:T(8,128)}, f32[256,256]{1,0:T(8,128)S(1)}, f32[256,256]{1,0:T(8,128)S(1)}, ...), branch_computations={%region_2.3_spmd, %region_3.4_spmd} | conditional | flops 12893552640 | bytes 87556200 | solution.py:146
  165.3 37.6 %collective-permute-start.2 = (f32[2,2,256,256]{2,3,0,1:T(8,128)}, f32[2,2,256,256]{2,3,0,1:T(8,128)}, u32[]{:S(2)}, u32[]{:S(2)}) collective-permute-start(f32[2,2,256,256]{2,3,0,1:T(8,128)} %get-tuple-element.1240), channel_id=1, source_target_pairs={{0,1},{1,2},{2,3},{4,5},{5,6},{6,7},{8,9},{9,10},{10,11},{12,13},{... | collective-permute-start | bytes 3145736 | tf_op jit(solution)/shard_map/ppermute | solution.py:20
  203.0 1.6 collective-permute-done.2
  204.6 9.0 %conditional.11 = (f32[2,2,2,256,256]{4,3,0,2,1:T(8,128)}, f32[2,2,256,256]{2,3,0,1:T(8,128)}) conditional(s32[]{:T(128)} %convert_element_type.664, (f32[2,2,256,256]{2,3,0,1:T(8,128)}, f32[2,2,2,256,256]{4,3,0,2,1:T(8,128)}) %tuple.90, (f32[2,2,256,256]{2,3,0,1:T(8,128)}, f32[256,256]{1,0:T(8,128)S(1)}, f32[256,256]{1,0:T(8,128)S(1)}, ...), branch_computations={%region_4.5_spmd, %region_5.6_spmd} | conditional | flops 12893552640 | bytes 87556200 | solution.py:146
  213.6 12.3 %collective-permute-start.3 = (f32[2,2,256,256]{2,3,0,1:T(8,128)}, f32[2,2,256,256]{2,3,0,1:T(8,128)}, u32[]{:S(2)}, u32[]{:S(2)}) collective-permute-start(f32[2,2,256,256]{2,3,0,1:T(8,128)} %get-tuple-element.1241), channel_id=1, source_target_pairs={{0,1},{1,2},{2,3},{4,5},{5,6},{6,7},{8,9},{9,10},{10,11},{12,13},{... | collective-permute-start | bytes 3145736 | tf_op jit(solution)/shard_map/ppermute | solution.py:20
  227.6 11.3 %conditional.12 = (f32[2,2,256,256]{3,2,0,1:T(8,128)}, f32[2,2,2,256,256]{4,3,0,2,1:T(8,128)}) conditional(s32[]{:T(128)} %convert_element_type.665, (f32[2,2,256,256]{2,3,0,1:T(8,128)}, f32[2,2,2,256,256]{4,3,0,2,1:T(8,128)}) %tuple.92, (f32[2,2,256,256]{2,3,0,1:T(8,128)}, f32[256,256]{1,0:T(8,128)S(1)}, f32[256,256]{1,0:T(8,128)S(1)}, ...), branch_computations={%region_6.7_spmd, %region_7.8_spmd} | conditional | flops 12893552640 | bytes 79167504 | solution.py:146
  227.6 2.5 copy.253
  238.9 11.2 %conditional.13 = (f32[2,2,256,256]{3,2,0,1:T(8,128)}) conditional(s32[]{:T(128)} %convert_element_type.665, () %tuple.86, (f32[2,2,256,256]{3,2,0,1:T(8,128)}, f32[256,256]{1,0:T(8,128)S(1)}, f32[256,256]{1,0:T(8,128)S(1)}, f32[256,256]{1,0:T(8,128)S(1)}, f32[256,256]{1,0:T(8,128)S(1)}, /*index=5*/f32[256,256]{1,0:T(8,128)S(1)}, ...), branch_computations={%region_8.9_spmd, %region_9.10_spmd} | conditional | flops 6445465600 | bytes 39845960 | solution.py:149
  250.1 17.2 %conditional.14 = (f32[2,2,256,256]{3,2,0,1:T(8,128)}, f32[2,2,2,256,256]{4,3,0,2,1:T(8,128)}) conditional(s32[]{:T(128)} %convert_element_type.665, f32[2,2,256,256]{3,2,0,1:T(8,128)} %get-tuple-element.1499, (f32[2,2,2,256,256]{4,3,2,1,0:T(8,128)S(1)}, f32[2,2,256,256]{3,2,0,1:T(8,128)}, f32[256,256]{1,0:T(8,128)S(1)}, ...), branch_computations={%region_10.11_spmd, %region_11.12_spmd} | conditional | flops 12895911936 | bytes 93323312 | solution.py:164
  250.2 1.5 broadcast.66
  267.3 1.3 collective-permute-start.4
  268.6 51.0 %collective-permute-done.4 = f32[2,2,256,256]{3,2,0,1:T(8,128)} collective-permute-done((f32[2,2,256,256]{3,2,0,1:T(8,128)}, f32[2,2,256,256]{3,2,0,1:T(8,128)}, u32[]{:S(2)}, u32[]{:S(2)}) %collective-permute-start.4) | collective-permute-done | bytes 1048608 | tf_op jit(solution)/shard_map/ppermute | solution.py:20
  319.6 8.8 %conditional.15 = ((f32[2,2,256,256]{3,2,0,1:T(8,128)}, f32[2,2,2,256,256]{4,3,0,2,1:T(8,128)})) conditional(s32[]{:T(128)} %convert_element_type.664, (f32[2,2,256,256]{3,2,0,1:T(8,128)}, f32[2,2,2,256,256]{4,3,0,2,1:T(8,128)}) %tuple.96, (f32[2,2,2,256,256]{4,3,2,1,0:T(8,128)S(1)}, f32[2,2,256,256]{3,2,0,1:T(8,128)}, f32[256,256]{1,0:T(8,128)S(1)}, ...), branch_computations={%region_12.13_spmd, %region_13.14_spmd} | conditional | flops 12895911936 | bytes 89128984 | solution.py:164
  328.4 1.3 collective-permute-start.5
  329.7 15.9 %collective-permute-done.5 = f32[2,2,256,256]{3,2,0,1:T(8,128)} collective-permute-done((f32[2,2,256,256]{3,2,0,1:T(8,128)}, f32[2,2,256,256]{3,2,0,1:T(8,128)}, u32[]{:S(2)}, u32[]{:S(2)}) %collective-permute-start.5) | collective-permute-done | bytes 1048608 | tf_op jit(solution)/shard_map/ppermute | solution.py:20
  345.6 8.8 %conditional.16 = ((f32[2,2,256,256]{3,2,0,1:T(8,128)}, f32[2,2,2,256,256]{4,3,0,2,1:T(8,128)})) conditional(s32[]{:T(128)} %convert_element_type.663, (f32[2,2,256,256]{3,2,0,1:T(8,128)}, f32[2,2,2,256,256]{4,3,0,2,1:T(8,128)}) %tuple.98, (f32[2,2,2,256,256]{4,3,2,1,0:T(8,128)S(1)}, f32[2,2,256,256]{3,2,0,1:T(8,128)}, f32[256,256]{1,0:T(8,128)S(1)}, ...), branch_computations={%region_14.15_spmd, %region_15.16_spmd} | conditional | flops 12895911936 | bytes 89128984 | solution.py:164
  354.3 1.3 collective-permute-start.6
  355.6 118.8 %collective-permute-done.6 = f32[2,2,256,256]{3,2,0,1:T(8,128)} collective-permute-done((f32[2,2,256,256]{3,2,0,1:T(8,128)}, f32[2,2,256,256]{3,2,0,1:T(8,128)}, u32[]{:S(2)}, u32[]{:S(2)}) %collective-permute-start.6) | collective-permute-done | bytes 1048608 | tf_op jit(solution)/shard_map/ppermute | solution.py:20
  474.4 22.1 %conditional.17 = (f32[2,2,2,256,256]{4,3,2,1,0:T(8,128)}) conditional(s32[]{:T(128)} %convert_element_type.662, f32[2,2,2,256,256]{4,3,0,2,1:T(8,128)} %get-tuple-element.877, (f32[2,2,2,256,256]{4,3,0,2,1:T(8,128)}, f32[2,2,2,256,256]{4,3,2,1,0:T(8,128)S(1)}, f32[2,2,256,256]{3,2,0,1:T(8,128)}, f32[256,256]{1,0:T(8,128)S(1)}, ...), branch_computations={%region_16.17_spmd, %region_17.18_spmd} | conditional | flops 6449266688 | bytes 56623112 | solution.py:164
  474.4 1.9 slice_bitcast_fusion.56
  476.4 1.5 multiply_add_fusion.57
  489.1 1.3 fusion.539
  494.7 1.5 copy.503
  496.5 4.4 broadcast_in_dim.6
  500.9 37.0 %while.14 = (s32[]{:T(128)}, f32[2,2,512,1024]{3,2,1,0:T(8,128)}, s32[2,2]{1,0:T(2,128)S(1)}, f32[2,2,2,256,256]{4,3,2,1,0:T(8,128)}, s32[]{:T(128)}, /*index=5*/s32[]{:T(128)}, s32[]{:T(128)}, s32[]{:T(128)}) while((s32[]{:T(128)}, f32[2,2,512,1024]{3,2,1,0:T(8,128)}, s32[2,2]{1,0:T(2,128)S(1)}, f32[2,2,2,256,256]{4,3,2,1,0:T(8,128)}, ...), condition=%wide.region_19.20_spmd, body=%wide.region_18.19_spmd.sunk | while | flops 262152 | bytes 5243077 | solution.py:175
  505.3 2.1 bitcast_add_fusion.2
  507.4 12.3 %dynamic_update_slice.8 = f32[2,2,512,1024]{3,2,1,0:T(8,128)} dynamic-update-slice(f32[2,2,512,1024]{3,2,1,0:T(8,128)} %get-tuple-element.1484, f32[2,2,256,256]{3,2,1,0:T(8,128)S(1)} %bitcast_add_fusion.2, s32[]{:T(128)} %constant.72.clone.1..sunk, s32[]{:T(128)} %constant.72.clone.1..sunk, s32[]{:T(128)S(6)} %select_n.700, s32[]{:T(128)S(6)} %select_n.701) | dynamic-update-slice | bytes 2097156 | tf_op jit(solution)/shard_map/while/body/eval_jaxpr/dynamic_update_slice | solution.py:173
  524.1 2.1 bitcast_add_fusion.2
  526.3 11.6 %dynamic_update_slice.8 = f32[2,2,512,1024]{3,2,1,0:T(8,128)} dynamic-update-slice(f32[2,2,512,1024]{3,2,1,0:T(8,128)} %get-tuple-element.1484, f32[2,2,256,256]{3,2,1,0:T(8,128)S(1)} %bitcast_add_fusion.2, s32[]{:T(128)} %constant.72.clone.1..sunk, s32[]{:T(128)} %constant.72.clone.1..sunk, s32[]{:T(128)S(6)} %select_n.700, s32[]{:T(128)S(6)} %select_n.701) | dynamic-update-slice | bytes 2097156 | tf_op jit(solution)/shard_map/while/body/eval_jaxpr/dynamic_update_slice | solution.py:173
  537.9 2.7 slice.290
  541.3 89.4 %collective-permute-done.7 = f32[2,2,256,1024]{3,2,1,0:T(8,128)S(1)} collective-permute-done((f32[2,2,256,1024]{3,2,1,0:T(8,128)S(1)}, f32[2,2,256,1024]{3,2,1,0:T(8,128)S(1)}, u32[]{:S(2)}, u32[]{:S(2)}) %collective-permute-start.7) | collective-permute-done | bytes 4194336 | tf_op jit(solution)/shard_map/ppermute | solution.py:14
  630.7 2.9 slice_add_fusion
  (79 shorter events, 53.0 us)
Async XLA Ops:
  0.0 8.4 %copy-start.11 = (s32[2,2]{1,0:T(2,128)S(1)}, s32[2,2]{1,0:T(2,128)}, u32[]{:S(2)}) copy-start(s32[2,2]{1,0:T(2,128)} %param.27) | copy-start | bytes 52
  0.0 95.2 %collective-permute-start = (f32[2,2,256,1024]{3,2,1,0:T(8,128)}, f32[2,2,256,1024]{3,2,1,0:T(8,128)}, u32[]{:S(2)}, u32[]{:S(2)}) collective-permute-start(f32[2,2,256,1024]{3,2,1,0:T(8,128)} %param.26), channel_id=1, source_target_pairs={{4,0},{8,4},{12,8},{0,12},{5,1},{9,5},{13,9},{1,13},{6,2},{10,6},{... | collective-permute-start | bytes 12582920 | tf_op jit(solution)/shard_map/ppermute | solution.py:14
  111.1 3.4 copy-start.1
  150.7 3.9 collective-permute-start.1
  165.3 39.3 %collective-permute-start.2 = (f32[2,2,256,256]{2,3,0,1:T(8,128)}, f32[2,2,256,256]{2,3,0,1:T(8,128)}, u32[]{:S(2)}, u32[]{:S(2)}) collective-permute-start(f32[2,2,256,256]{2,3,0,1:T(8,128)} %get-tuple-element.1240), channel_id=1, source_target_pairs={{0,1},{1,2},{2,3},{4,5},{5,6},{6,7},{8,9},{9,10},{10,11},{12,13},{... | collective-permute-start | bytes 3145736 | tf_op jit(solution)/shard_map/ppermute | solution.py:20
  213.6 14.0 %collective-permute-start.3 = (f32[2,2,256,256]{2,3,0,1:T(8,128)}, f32[2,2,256,256]{2,3,0,1:T(8,128)}, u32[]{:S(2)}, u32[]{:S(2)}) collective-permute-start(f32[2,2,256,256]{2,3,0,1:T(8,128)} %get-tuple-element.1241), channel_id=1, source_target_pairs={{0,1},{1,2},{2,3},{4,5},{5,6},{6,7},{8,9},{9,10},{10,11},{12,13},{... | collective-permute-start | bytes 3145736 | tf_op jit(solution)/shard_map/ppermute | solution.py:20
  267.3 52.3 %collective-permute-start.4 = (f32[2,2,256,256]{3,2,0,1:T(8,128)}, f32[2,2,256,256]{3,2,0,1:T(8,128)}, u32[]{:S(2)}, u32[]{:S(2)}) collective-permute-start(f32[2,2,256,256]{3,2,0,1:T(8,128)} %get-tuple-element.873), channel_id=1, source_target_pairs={{1,0},{2,1},{3,2},{5,4},{6,5},{7,6},{9,8},{10,9},{11,10},{13,12},{... | collective-permute-start | bytes 3145736 | tf_op jit(solution)/shard_map/ppermute | solution.py:20
  328.4 17.2 %collective-permute-start.5 = (f32[2,2,256,256]{3,2,0,1:T(8,128)}, f32[2,2,256,256]{3,2,0,1:T(8,128)}, u32[]{:S(2)}, u32[]{:S(2)}) collective-permute-start(f32[2,2,256,256]{3,2,0,1:T(8,128)} %get-tuple-element.875), channel_id=1, source_target_pairs={{1,0},{2,1},{3,2},{5,4},{6,5},{7,6},{9,8},{10,9},{11,10},{13,12},{... | collective-permute-start | bytes 3145736 | tf_op jit(solution)/shard_map/ppermute | solution.py:20
  354.3 120.1 %collective-permute-start.6 = (f32[2,2,256,256]{3,2,0,1:T(8,128)}, f32[2,2,256,256]{3,2,0,1:T(8,128)}, u32[]{:S(2)}, u32[]{:S(2)}) collective-permute-start(f32[2,2,256,256]{3,2,0,1:T(8,128)} %get-tuple-element.878), channel_id=1, source_target_pairs={{1,0},{2,1},{3,2},{5,4},{6,5},{7,6},{9,8},{10,9},{11,10},{13,12},{... | collective-permute-start | bytes 3145736 | tf_op jit(solution)/shard_map/ppermute | solution.py:20
  496.4 4.4 copy-start.12
  537.9 92.9 %copy-start = (f32[2,2,512,1024]{3,2,1,0:T(8,128)S(1)}, f32[2,2,512,1024]{3,2,1,0:T(8,128)}, u32[]{:S(2)}) copy-start(f32[2,2,512,1024]{3,2,1,0:T(8,128)} %get-tuple-element.879) | copy-start | bytes 25165828
  540.5 90.2 %collective-permute-start.7 = (f32[2,2,256,1024]{3,2,1,0:T(8,128)S(1)}, f32[2,2,256,1024]{3,2,1,0:T(8,128)S(1)}, u32[]{:S(2)}, u32[]{:S(2)}) collective-permute-start(f32[2,2,256,1024]{3,2,1,0:T(8,128)S(1)} %slice.290), channel_id=1, source_target_pairs={{12,0},{0,4},{4,8},{8,12},{13,1},{1,5},{5,9},{9,13},{14,2},{2,6},{... | collective-permute-start | bytes 12582920 | tf_op jit(solution)/shard_map/ppermute | solution.py:14
where the time goes:
time: 640 us; the launch traced here: 634 us
  waiting for transfers between devices  365 us (57%)
  loops' own time  80.7 us (13%)
  starting transfers between devices  62 us (10%)
  local copies, waits for them, and re-layouts  52.8 us (8%)
  matrix products  50 us (8%)
  other arithmetic  22.5 us (4%)
    ppermute x6, waiting for transfers between devices, passed_along(): return lax.ppermute(block, axis, route)  190 us
    ppermute x2, waiting for transfers between devices, shifted(): return lax.ppermute(block, axis, route)  175 us
    ppermute x6, starting transfers between devices, passed_along(): return lax.ppermute(block, axis, route)  56.1 us
    another operation x4, loops' own time, body(): lax.cond(depth_index == step_number, retreat, keeping, (chi_wave, terms))  33.7 us
    another operation x4, loops' own time, body(): lax.cond(depth_index == step_number, advance, passing, (wave_now, saved))  29.2 us
    dot_general x24, matrix products, left_product(): jnp.einsum('jk,...kl->...jl', matrix, field, preferred_element_type=jnp.f...  25.5 us
    dot_general x24, matrix products, right_product(): jnp.einsum('...jk,kl->...jl', field, matrix, preferred_element_type=jnp.f...  24.6 us
    dynamic_update_slice x2, local copies, waits for them, and re-layouts, add_slot(): lax.dynamic_update_slice(grad_now, current + terms[slot_index], start)  23.9 us
  transfers between devices with their start and end apart: 8, of which 8 were waited for; matrix products, arithmetic and copies ran while one was open for 1% of the time, Pallas kernels for 0%

commit v1 on v0

v1 whole, which is shorter than its diff:
```python
import functools
import math

import jax
import jax.numpy as jnp
import numpy as np
from jax import lax
from jax.experimental import pallas as pl
from jax.experimental.pallas import tpu as pltpu
from jax.sharding import PartitionSpec as P

chirp_rate = 0.25
CHUNK = 32


def make_tables(length):
    index = np.arange(length)
    angle = 2.0 * np.pi / length * (index[:, None] * index[None, :] % length)
    forward = (np.cos(angle) - 1j * np.sin(angle)) / math.sqrt(length)
    freq = np.where(index < length // 2, index, index - length).astype(np.float64)
    chirp = np.exp(-1j * np.pi * chirp_rate / length * freq**2)
    step = (np.conj(forward) * chirp[None, :]) @ forward
    left_hi, left_lo, right_hi, right_lo = [], [], [], []
    for table in (step, forward):
        real, imag = table.real, table.imag
        left = np.block([[real, -imag], [imag, real]]).astype(np.float32)
        right = np.block([[real, imag], [-imag, real]]).astype(np.float32)
        for whole, highs, lows in ((left, left_hi, left_lo), (right, right_hi, right_lo)):
            high = whole.astype(jnp.bfloat16)
            highs.append(high)
            lows.append((whole - high.astype(np.float32)).astype(jnp.bfloat16))
    return tuple(np.stack(parts) for parts in (left_hi, left_lo, right_hi, right_lo))


def dot(a, b):
    return jnp.dot(a, b, preferred_element_type=jnp.float32)


def split(x):
    high = x.astype(jnp.bfloat16)
    low = (x - high.astype(jnp.float32)).astype(jnp.bfloat16)
    return high, low


def kernel(
    tiles, groups,
    probe, slices, pos, amp, live, left_hi, left_lo, right_hi, right_lo,
    out,
    pieces, win, nbr, psi, wave_in, wave_out, chi_in, chi_out, terms, terms_in, pos_in, cur,
    pos_sem, piece_send, piece_recv, wave_send, wave_recv, chi_send, chi_recv, term_send, term_recv,
):
    slots, layers, _, size, _ = pieces.shape
    blocks = slices.shape[-1] // size
    tile = lax.axis_index("scan")
    group = lax.axis_index("depth")
    last = groups - 1
    next_tile = lax.rem(tile + 1, tiles)
    prev_tile = lax.rem(tile + tiles - 1, tiles)
    next_group = lax.rem(group + 1, groups)
    prev_group = lax.rem(group + groups - 1, groups)

    def remote(src, dst, send, recv, where):
        return pltpu.make_async_remote_copy(
            src_ref=src, dst_ref=dst, send_sem=send, recv_sem=recv,
            device_id=where, device_id_type=pl.DeviceIdType.MESH,
        )

    def piece_copy(s, l):
        return remote(pieces.at[s, l], nbr.at[s, l], piece_send.at[s, l], piece_recv.at[s, l], {"scan": prev_tile})

    def term_copy(s, l):
        return remote(terms.at[s, l], terms_in.at[s, l], term_send.at[s, l], term_recv.at[s, l], {"scan": next_tile})

    def wave_copy(s):
        return remote(wave_out.at[s], wave_in.at[s], wave_send.at[s], wave_recv.at[s], {"depth": next_group})

    def chi_copy(s):
        return remote(chi_out.at[s], chi_in.at[s], chi_send.at[s], chi_recv.at[s], {"depth": prev_group})

    barrier = pltpu.get_barrier_semaphore()
    for where in ({"scan": next_tile}, {"scan": prev_tile}, {"depth": next_group}, {"depth": prev_group}):
        pl.semaphore_signal(barrier, inc=1, device_id=where, device_id_type=pl.DeviceIdType.MESH)
    pl.semaphore_wait(barrier, 4)

    pos_copy = remote(pos, pos_in, pos_sem.at[0], pos_sem.at[1], {"scan": next_tile})
    pos_copy.start()

    def rows_of(chunk):
        return pl.ds(pl.multiple_of(chunk * CHUNK, CHUNK), CHUNK)

    def iotas(chunk):
        row = lax.broadcasted_iota(jnp.int32, (CHUNK, size), 0) + chunk * CHUNK
        column = lax.broadcasted_iota(jnp.int32, (CHUNK, size), 1)
        return row, column

    def inside(column, block, start):
        offset = column + block * size - start
        return (offset >= 0) & (offset < size)

    def cut(places, target, s, l, own):
        def one(chunk, carry):
            row, column = iotas(chunk)
            keep = row >= places[s, 0, 0:1, :]
            if not own:
                keep = jnp.logical_not(keep)
            start = places[s, 1, 0:1, :]
            for part in range(2):
                value = jnp.zeros((CHUNK, size), jnp.float32)
                for block in range(blocks):
                    value = jnp.where(
                        inside(column, block, start),
                        slices[l, part, rows_of(chunk), block * size : (block + 1) * size],
                        value,
                    )
                target[s, l, part, rows_of(chunk), :] = jnp.where(keep, value, 0.0)
            return carry

        lax.fori_loop(0, size // CHUNK, one, 0)

    def add_terms(places, source, s, l, own):
        def one(chunk, carry):
            row, column = iotas(chunk)
            keep = row >= places[s, 0, 0:1, :]
            if not own:
                keep = jnp.logical_not(keep)
            start = places[s, 1, 0:1, :]
            for part in range(2):
                value = jnp.where(keep, source[s, l, part, rows_of(chunk), :], 0.0)
                for block in range(blocks):
                    out[l, part, rows_of(chunk), block * size : (block + 1) * size] += jnp.where(
                        inside(column, block, start), value, 0.0
                    )
            return carry

        lax.fori_loop(0, size // CHUNK, one, 0)

    def two_sided(which, real, imag):
        high, low = split(jnp.concatenate([real, imag], axis=1))
        y = dot(high, right_hi[which]) + dot(high, right_lo[which]) + dot(low, right_hi[which])
        high, low = split(jnp.concatenate([y[:, :size], y[:, size:]], axis=0))
        z = dot(left_hi[which], high) + dot(left_lo[which], high) + dot(left_hi[which], low)
        return z[:size], z[size:]

    pos_copy.wait_recv()

    for s in range(slots):
        for l in range(layers):
            cut(pos_in, pieces, s, l, False)
            piece_copy(s, l).start()

    out[...] = jnp.zeros_like(out)
    for s in range(slots):
        for l in range(layers):
            cut(pos, win, s, l, True)

    def roll_probe(s):
        row = lax.broadcasted_iota(jnp.int32, (size, size), 0)
        column = lax.broadcasted_iota(jnp.int32, (size, size), 1)
        down = row - column - pos[s, 0, 0:1, :]
        across = column - row - pos[s, 1, 0:1, :]
        rows_shift = jnp.zeros((size, size), jnp.float32)
        for turn in range(2):
            rows_shift = jnp.where(down == -turn * size, 1.0, rows_shift)
        columns_shift = jnp.zeros((size, size), jnp.float32)
        for turn in range(blocks + 1):
            columns_shift = jnp.where(across == -turn * size, 1.0, columns_shift)
        rows_shift = rows_shift.astype(jnp.bfloat16)
        columns_shift = columns_shift.astype(jnp.bfloat16)

        def three(x):
            first = x.astype(jnp.bfloat16)
            rest = x - first.astype(jnp.float32)
            second = rest.astype(jnp.bfloat16)
            third = (rest - second.astype(jnp.float32)).astype(jnp.bfloat16)
            return first, second, third

        for part in range(2):
            a, b, c = three(probe[part])
            x = dot(rows_shift, a) + dot(rows_shift, b) + dot(rows_shift, c)
            a, b, c = three(x)
            wave_in[s, part] = dot(a, columns_shift) + dot(b, columns_shift) + dot(c, columns_shift)

    def forward(s):
        @pl.when(group == 0)
        def _():
            roll_probe(s)

        @pl.when(group > 0)
        def _():
            wave_copy(s).wait_recv()

        for l in range(layers):
            source = wave_in.at[s] if l == 0 else cur
            real, imag = two_sided(0, source[0], source[1])
            psi[s, l, 0] = real
            psi[s, l, 1] = imag
            piece_copy(s, l).wait_recv()
            real, imag = psi[s, l, 0], psi[s, l, 1]
            w_real = win[s, l, 0] + nbr[s, l, 0]
            w_imag = win[s, l, 1] + nbr[s, l, 1]
            target = cur if l < layers - 1 else wave_out.at[s]
            target[0] = real * w_real - imag * w_imag
            target[1] = real * w_imag + imag * w_real

        @pl.when(group < last)
        def _():
            wave_copy(s).start()

        @pl.when(group == last)
        def _():
            real, imag = two_sided(1, wave_out[s, 0], wave_out[s, 1])
            keep = live[s, 0:1, :] * (1.0 - amp[s] / jnp.sqrt(real * real + imag * imag + 1.0))
            cur[0] = real * keep
            cur[1] = -(imag * keep)
            real, imag = two_sided(1, cur[0], cur[1])
            chi_in[s, 0] = real
            chi_in[s, 1] = imag

    def adjoint(s):
        @pl.when(group < last)
        def _():
            chi_copy(s).wait_recv()

        for l in range(layers - 1, -1, -1):
            source = chi_in.at[s] if l == layers - 1 else cur
            c_real, c_imag = source[0], source[1]
            terms[s, l, 0] = psi[s, l, 0] * c_real - psi[s, l, 1] * c_imag
            terms[s, l, 1] = -(psi[s, l, 0] * c_imag + psi[s, l, 1] * c_real)
            term_copy(s, l).start()

            def back():
                w_real = win[s, l, 0] + nbr[s, l, 0]
                w_imag = win[s, l, 1] + nbr[s, l, 1]
                c_real, c_imag = source[0], source[1]
                return two_sided(0, w_real * c_real - w_imag * c_imag, w_real * c_imag + w_imag * c_real)

            if l > 0:
                real, imag = back()
                cur[0] = real
                cur[1] = imag
            else:

                @pl.when(group > 0)
                def _():
                    real, imag = back()
                    chi_out[s, 0] = real
                    chi_out[s, 1] = imag
                    chi_copy(s).start()

        for l in range(layers):
            add_terms(pos, terms, s, l, True)

    def task(k, carry):
        at_last = group == last
        is_forward = jnp.where(at_last, lax.rem(k, 2) == 0, k < slots)
        s = jnp.where(at_last, k // 2, lax.rem(k, slots))

        @pl.when(is_forward)
        def _():
            forward(s)

        @pl.when(jnp.logical_not(is_forward))
        def _():
            adjoint(s)

        return carry

    lax.fori_loop(0, 2 * slots, task, 0)

    for s in range(slots):
        for l in range(layers - 1, -1, -1):
            term_copy(s, l).wait_recv()
            add_terms(pos_in, terms_in, s, l, False)

    pos_copy.wait_send()
    for s in range(slots):
        for l in range(layers):
            piece_copy(s, l).wait_send()
            term_copy(s, l).wait_send()

    @pl.when(group < last)
    def _():
        for s in range(slots):
            wave_copy(s).wait_send()

    @pl.when(group > 0)
    def _():
        for s in range(slots):
            chi_copy(s).wait_send()


def solution(mesh):
    tiles, groups = mesh.shape["scan"], mesh.shape["depth"]

    def body(probe, slices, positions, counts, amplitude):
        size = probe.shape[-1]
        slots = positions.shape[0]
        layers = slices.shape[0]
        places = jnp.broadcast_to(positions[:, :, None, None], (slots, 2, 8, size))
        live = (jnp.arange(slots, dtype=jnp.int32) < counts[0]).astype(jnp.float32)
        live = jnp.broadcast_to(live[:, None, None], (slots, 8, size))
        tables = [jnp.asarray(table) for table in make_tables(size)]
        planes = pltpu.VMEM((slots, layers, 2, size, size), jnp.float32)
        waves = pltpu.VMEM((slots, 2, size, size), jnp.float32)
        each = pltpu.SemaphoreType.DMA((slots, layers))
        some = pltpu.SemaphoreType.DMA((slots,))
        return pl.pallas_call(
            functools.partial(kernel, tiles, groups),
            out_shape=jax.ShapeDtypeStruct(slices.shape, jnp.float32),
            in_specs=[pl.BlockSpec(memory_space=pltpu.VMEM)] * 9,
            out_specs=pl.BlockSpec(memory_space=pltpu.VMEM),
            scratch_shapes=[
                planes, planes, planes, planes,
                waves, waves, waves, waves,
                planes, planes,
                pltpu.VMEM((slots, 2, 8, size), jnp.int32),
                pltpu.VMEM((2, size, size), jnp.float32),
                pltpu.SemaphoreType.DMA((2,)),
                each, each, some, some, some, some, each, each,
            ],
            compiler_params=pltpu.CompilerParams(
                collective_id=0, has_side_effects=True, vmem_limit_bytes=52 * 1024 * 1024
            ),
        )(probe, slices, places, amplitude, live, *tables)

    return jax.shard_map(
        body,
        mesh=mesh,
        in_specs=(
            P(),
            P("depth", None, ("groups", "scan"), None),
            P(("groups", "scan"), None),
            P(("groups", "scan")),
            P(("groups", "scan"), None, None),
        ),
        out_specs=P("depth", None, ("groups", "scan"), None),
        check_vma=False,
    )
```

time: 640 us -> 144 us (0.23)
  waiting for transfers between devices: 365 us -> 0 us
  Pallas kernels: 0 us -> 136 us
  loops' own time: 80.7 us -> 0 us
  starting transfers between devices: 62 us -> 0 us
  matrix products: 50 us -> 0 us
  local copies, waits for them, and re-layouts: 52.8 us -> 7.69 us
  other arithmetic: 22.5 us -> 0.01 us
    ppermute x8 -> x0, waiting for transfers between devices: 365 us -> none  [the longest x6 190 us: passed_along(): return lax.ppermute(block, axis, route)]
    pallas_call x0 -> x1, Pallas kernels: none -> 136 us  [body(): pl.pallas_call(functools.partial(kernel, tiles, groups), out_shape=jax.Sh...]
    another operation x11 -> x0, loops' own time: 80.7 us -> none  [the longest x4 33.7 us: body(): lax.cond(depth_index == step_number, retreat, keeping, (chi_wave, terms))]
    ppermute x8 -> x0, starting transfers between devices: 62 us -> none  [the longest x6 56.1 us: passed_along(): return lax.ppermute(block, axis, route)]
    dot_general x48 -> x0, matrix products: 50 us -> none  [the longest x24 25.5 us: left_product(): jnp.einsum('jk,...kl->...jl', matrix, field, preferred_element_type=jnp.f...]
    dynamic_update_slice x2 -> x0, local copies, waits for them, and re-layouts: 23.9 us -> none  [add_slot(): lax.dynamic_update_slice(grad_now, current + terms[slot_index], start)]
    add x4 -> x0, other arithmetic: 8.72 us -> none  [the longest x2 4.24 us: add_slot(): current + terms[slot_index]]
    concatenate x2 -> x0, other arithmetic: 8.54 us -> none  [the longest x1 8.47 us: body(): extended = jnp.concatenate([slices, neighbour], axis=2)]
  transfers between devices with their start and end apart: 8 -> 0, of which waited for: 8 -> 0; matrix products, arithmetic and copies ran while one was open for 1% -> 0% of each run, Pallas kernels for 0% -> 0%
where the time goes in v1:
time: 144 us
  Pallas kernels  136 us (94%)
  local copies, waits for them, and re-layouts  7.69 us (5%)
    pallas_call x1, Pallas kernels, body(): pl.pallas_call(functools.partial(kernel, tiles, groups), out_shape=jax.Sh...  136 us
    unnamed x5, local copies, waits for them, and re-layouts  6.87 us

profile of v1, /device:TPU:0, one launch (start us, length us, event | category | flops | bytes accessed | tf_op | source)
XLA Modules:
  0.0 144.0 jit_solution(7507992398323292447)
XLA Ops:
  0.7 0.1 broadcast_in_dim.5.live
  0.7 0.8 broadcast_in_dim.4.pos
  1.5 0.0 copy-start
  1.5 1.0 copy-done
  2.5 0.0 copy-start.1
  2.5 1.0 copy-done.1
  3.6 135.7 %shard_map.91 = f32[2,2,256,1024]{3,2,1,0:T(8,128)} custom-call(f32[2,256,256]{2,1,0:T(8,128)S(1)} %copy-done, f32[2,2,256,1024]{3,2,1,0:T(8,128)} %slices.1, s32[2,2,8,256]{3,2,1,0:T(8,128)S(1)} %broadcast_in_dim.4.pos, f32[2,256,256]{2,1,0:T(8,128)S(1)} %copy-done.1, f32[2,8,256]{2,1,0:T(8,128)S(1)} %broadcast_in_dim.5.live, ...), custom_call_target="tpu_custom_call" | custom-call | tf_op jit(solution)/shard_map/pallas_call | solution.py:307
  139.2 4.8 %copy.12 = f32[2,2,256,1024]{3,2,1,0:T(8,128)} copy(f32[2,2,256,1024]{3,2,1,0:T(8,128)} %shard_map.91) | data formatting | bytes 8388608
  (1 shorter events, 0.0 us)
Async XLA Ops:
  1.5 1.0 copy-start
  2.5 1.0 copy-start.1

commit v2 on v1

--- a/solution.py
+++ b/solution.py
@@ -146,7 +146,8 @@
     for s in range(slots):
         for l in range(layers):
             cut(pos_in, pieces, s, l, False)
-            piece_copy(s, l).start()
+            if s == 0:
+                piece_copy(s, l).start()
 
     out[...] = jnp.zeros_like(out)
     for s in range(slots):
@@ -180,20 +181,34 @@
             a, b, c = three(x)
             wave_in[s, part] = dot(a, columns_shift) + dot(b, columns_shift) + dot(c, columns_shift)
 
+    def first_psi(s, carry):
+        roll_probe(s)
+        propagate(wave_in.at[s], s, 0)
+        return carry
+
+    def propagate(source, s, l):
+        real, imag = two_sided(0, source[0], source[1])
+        psi[s, l, 0] = real
+        psi[s, l, 1] = imag
+
+    @pl.when(group == 0)
+    def _():
+        lax.fori_loop(0, slots, first_psi, 0)
+
+    for s in range(1, slots):
+        for l in range(layers):
+            piece_copy(s - 1, l).wait_send()
+            piece_copy(s, l).start()
+
     def forward(s):
-        @pl.when(group == 0)
-        def _():
-            roll_probe(s)
-
         @pl.when(group > 0)
         def _():
             wave_copy(s).wait_recv()
-
-        for l in range(layers):
-            source = wave_in.at[s] if l == 0 else cur
-            real, imag = two_sided(0, source[0], source[1])
-            psi[s, l, 0] = real
-            psi[s, l, 1] = imag
+            propagate(wave_in.at[s], s, 0)
+
+        for l in range(layers):
+            if l > 0:
+                propagate(cur, s, l)
             piece_copy(s, l).wait_recv()
             real, imag = psi[s, l, 0], psi[s, l, 1]
             w_real = win[s, l, 0] + nbr[s, l, 0]
@@ -251,7 +266,7 @@
             add_terms(pos, terms, s, l, True)
 
     def task(k, carry):
-        at_last = group == last
+        at_last = group * 2 >= groups
         is_forward = jnp.where(at_last, lax.rem(k, 2) == 0, k < slots)
         s = jnp.where(at_last, k // 2, lax.rem(k, slots))
 
@@ -275,7 +290,8 @@
     pos_copy.wait_send()
     for s in range(slots):
         for l in range(layers):
-            piece_copy(s, l).wait_send()
+            if s == slots - 1:
+                piece_copy(s, l).wait_send()
             term_copy(s, l).wait_send()
 
     @pl.when(group < last)

time: 144 us -> 132 us (0.917)
  Pallas kernels: 136 us -> 124 us
    pallas_call x1, Pallas kernels: 136 us -> 124 us  [body(): pl.pallas_call(functools.partial(kernel, tiles, groups), out_shape=jax.Sh...]
where the time goes in v2:
time: 132 us
  Pallas kernels  124 us (94%)
  local copies, waits for them, and re-layouts  7.69 us (6%)
    pallas_call x1, Pallas kernels, body(): pl.pallas_call(functools.partial(kernel, tiles, groups), out_shape=jax.Sh...  124 us
    unnamed x5, local copies, waits for them, and re-layouts  6.87 us

profile of v2, /device:TPU:0, one launch (start us, length us, event | category | flops | bytes accessed | tf_op | source)
XLA Modules:
  0.0 131.9 jit_solution(12153938876032756052)
XLA Ops:
  0.7 0.1 broadcast_in_dim.5.live
  0.7 0.8 broadcast_in_dim.4.pos
  1.5 0.0 copy-start
  1.5 1.0 copy-done
  2.5 0.0 copy-start.1
  2.5 1.0 copy-done.1
  3.6 123.5 %shard_map.91 = f32[2,2,256,1024]{3,2,1,0:T(8,128)} custom-call(f32[2,256,256]{2,1,0:T(8,128)S(1)} %copy-done, f32[2,2,256,1024]{3,2,1,0:T(8,128)} %slices.1, s32[2,2,8,256]{3,2,1,0:T(8,128)S(1)} %broadcast_in_dim.4.pos, f32[2,256,256]{2,1,0:T(8,128)S(1)} %copy-done.1, f32[2,8,256]{2,1,0:T(8,128)S(1)} %broadcast_in_dim.5.live, ...), custom_call_target="tpu_custom_call" | custom-call | tf_op jit(solution)/shard_map/pallas_call | solution.py:323
  127.1 4.8 %copy.12 = f32[2,2,256,1024]{3,2,1,0:T(8,128)} copy(f32[2,2,256,1024]{3,2,1,0:T(8,128)} %shard_map.91) | data formatting | bytes 8388608
  (1 shorter events, 0.0 us)
Async XLA Ops:
  1.5 1.0 copy-start
  2.5 1.0 copy-start.1

commit v3 on v2

--- a/solution.py
+++ b/solution.py
@@ -136,9 +136,12 @@
 
     def two_sided(which, real, imag):
         high, low = split(jnp.concatenate([real, imag], axis=1))
-        y = dot(high, right_hi[which]) + dot(high, right_lo[which]) + dot(low, right_hi[which])
+        both = dot(jnp.concatenate([high, low], axis=0), right_hi[which])
+        y = both[:size] + both[size:] + dot(high, right_lo[which])
         high, low = split(jnp.concatenate([y[:, :size], y[:, size:]], axis=0))
-        z = dot(left_hi[which], high) + dot(left_lo[which], high) + dot(left_hi[which], low)
+        left = jnp.concatenate([left_hi[which], left_lo[which]], axis=0)
+        both = dot(left, high)
+        z = both[: 2 * size] + both[2 * size :] + dot(left_hi[which], low)
         return z[:size], z[size:]
 
     pos_copy.wait_recv()
@@ -262,9 +265,6 @@
                     chi_out[s, 1] = imag
                     chi_copy(s).start()
 
-        for l in range(layers):
-            add_terms(pos, terms, s, l, True)
-
     def task(k, carry):
         at_last = group * 2 >= groups
         is_forward = jnp.where(at_last, lax.rem(k, 2) == 0, k < slots)
@@ -282,6 +282,9 @@
 
     lax.fori_loop(0, 2 * slots, task, 0)
 
+    for s in range(slots):
+        for l in range(layers - 1, -1, -1):
+            add_terms(pos, terms, s, l, True)
     for s in range(slots):
         for l in range(layers - 1, -1, -1):
             term_copy(s, l).wait_recv()

time: 132 us -> 135 us (1.023)
  Pallas kernels: 124 us -> 126 us
    pallas_call x1, Pallas kernels: 124 us -> 126 us  [body(): pl.pallas_call(functools.partial(kernel, tiles, groups), out_shape=jax.Sh...]
where the time goes in v3:
time: 135 us
  Pallas kernels  126 us (93%)
  local copies, waits for them, and re-layouts  7.69 us (6%)
    pallas_call x1, Pallas kernels, body(): pl.pallas_call(functools.partial(kernel, tiles, groups), out_shape=jax.Sh...  126 us
    unnamed x5, local copies, waits for them, and re-layouts  6.87 us

profile of v3, /device:TPU:0, one launch (start us, length us, event | category | flops | bytes accessed | tf_op | source)
XLA Modules:
  0.0 134.5 jit_solution(2481884906499601822)
XLA Ops:
  0.7 0.1 broadcast_in_dim.5.live
  0.7 0.8 broadcast_in_dim.4.pos
  1.5 0.0 copy-start
  1.5 1.0 copy-done
  2.5 0.0 copy-start.1
  2.5 1.0 copy-done.1
  3.6 126.2 %shard_map.91 = f32[2,2,256,1024]{3,2,1,0:T(8,128)} custom-call(f32[2,256,256]{2,1,0:T(8,128)S(1)} %copy-done, f32[2,2,256,1024]{3,2,1,0:T(8,128)} %slices.1, s32[2,2,8,256]{3,2,1,0:T(8,128)S(1)} %broadcast_in_dim.4.pos, f32[2,256,256]{2,1,0:T(8,128)S(1)} %copy-done.1, f32[2,8,256]{2,1,0:T(8,128)S(1)} %broadcast_in_dim.5.live, ...), custom_call_target="tpu_custom_call" | custom-call | tf_op jit(solution)/shard_map/pallas_call | solution.py:326
  129.8 4.8 %copy.12 = f32[2,2,256,1024]{3,2,1,0:T(8,128)} copy(f32[2,2,256,1024]{3,2,1,0:T(8,128)} %shard_map.91) | data formatting | bytes 8388608
  (1 shorter events, 0.0 us)
Async XLA Ops:
  1.5 1.0 copy-start
  2.5 1.0 copy-start.1

commit v4 on v3

--- a/solution.py
+++ b/solution.py
@@ -265,6 +265,9 @@
                     chi_out[s, 1] = imag
                     chi_copy(s).start()
 
+        for l in range(layers):
+            add_terms(pos, terms, s, l, True)
+
     def task(k, carry):
         at_last = group * 2 >= groups
         is_forward = jnp.where(at_last, lax.rem(k, 2) == 0, k < slots)
@@ -282,9 +285,6 @@
 
     lax.fori_loop(0, 2 * slots, task, 0)
 
-    for s in range(slots):
-        for l in range(layers - 1, -1, -1):
-            add_terms(pos, terms, s, l, True)
     for s in range(slots):
         for l in range(layers - 1, -1, -1):
             term_copy(s, l).wait_recv()

time: 135 us -> 135 us (level)
  no operation moved by 1% of the time
where the time goes in v4:
time: 135 us
  Pallas kernels  126 us (93%)
  local copies, waits for them, and re-layouts  7.69 us (6%)
    pallas_call x1, Pallas kernels, body(): pl.pallas_call(functools.partial(kernel, tiles, groups), out_shape=jax.Sh...  126 us
    unnamed x5, local copies, waits for them, and re-layouts  6.87 us

profile of v4, /device:TPU:0, one launch (start us, length us, event | category | flops | bytes accessed | tf_op | source)
XLA Modules:
  0.0 134.5 jit_solution(73059831714825217)
XLA Ops:
  0.7 0.1 broadcast_in_dim.5.live
  0.7 0.8 broadcast_in_dim.4.pos
  1.5 0.0 copy-start
  1.5 1.0 copy-done
  2.5 0.0 copy-start.1
  2.5 1.0 copy-done.1
  3.6 126.2 %shard_map.91 = f32[2,2,256,1024]{3,2,1,0:T(8,128)} custom-call(f32[2,256,256]{2,1,0:T(8,128)S(1)} %copy-done, f32[2,2,256,1024]{3,2,1,0:T(8,128)} %slices.1, s32[2,2,8,256]{3,2,1,0:T(8,128)S(1)} %broadcast_in_dim.4.pos, f32[2,256,256]{2,1,0:T(8,128)S(1)} %copy-done.1, f32[2,8,256]{2,1,0:T(8,128)S(1)} %broadcast_in_dim.5.live, ...), custom_call_target="tpu_custom_call" | custom-call | tf_op jit(solution)/shard_map/pallas_call | solution.py:326
  129.8 4.8 %copy.12 = f32[2,2,256,1024]{3,2,1,0:T(8,128)} copy(f32[2,2,256,1024]{3,2,1,0:T(8,128)} %shard_map.91) | data formatting | bytes 8388608
  (1 shorter events, 0.0 us)
Async XLA Ops:
  1.5 1.0 copy-start
  2.5 1.0 copy-start.1
